TPU v7x, 512 devices: a whole 4x8x8 slice. The times are simulated.
512 devices in a mesh: lat: 16 (over z, core), lon: 8 (over y), hid: 4 (over x).
Axes of the slice: x: 4, y: 8, z: 8, core: 2. Of those that a mesh axis runs over, the one named last changes fastest.
Arguments:
- grid_latent: float32 [128, 1024, 512], P('lat', 'lon'), may hold values from -6 to 6
- mesh_latent: float32 [16, 8, 512, 512], P('lat', 'lon'), may hold values from -6 to 6
- grid_edge_feats: float32 [16, 8, 4, 1024], P('lat', 'lon'), may hold values from -6 to 6
- grid_senders: int32 [16, 8, 1024], P('lat', 'lon'), may hold values from 0 to 131071, as said below
- grid_receivers: int32 [16, 8, 1024], P('lat', 'lon'), may hold values from -1 to 65535, as said below
- mesh_edge_feats: float32 [16, 8, 4, 512], P('lat', 'lon'), may hold values from -6 to 6
- mesh_senders: int32 [16, 8, 512], P('lat', 'lon'), may hold values from 0 to 65535, as said below
- mesh_receivers: int32 [16, 8, 512], P('lat', 'lon'), may hold values from -1 to 65535, as said below
- edge_weight: float32 [2, 4, 512], P(None, None, 'hid'), may hold values from -1.75 to 1.75
- sender_weight: float32 [2, 512, 512], P(None, None, 'hid'), may hold values from -0.15625 to 0.15625
- receiver_weight: float32 [2, 512, 512], P(None, None, 'hid'), may hold values from -0.15625 to 0.15625
- first_bias: float32 [2, 512], P(None, 'hid'), may hold values from -1 to 1
- out_weight: float32 [2, 512, 512], P(None, 'hid'), may hold values from -4 to 4
- out_bias: float32 [2, 512], replicated, may hold values from -3 to 3
- norm_gain: float32 [2, 512], replicated, may hold values from 0.5 to 1.5
- norm_shift: float32 [2, 512], replicated, may hold values from -3 to 3
Outputs:
- mesh_out: float32 [16, 8, 512, 512], P('lat', 'lon', None, 'hid')
Inputs may be any that keep to these rules, and one draw needn't show every extreme that they name: `grid_senders`: A live slot of patch (a, b) sends from a grid cell of block (a, b) or within 2 cells outside it in latitude (never past the first or last row) and in longitude (wrapping round); a padding slot names the first cell of its own block. `grid_receivers`: in each patch's block of 1024 slots the live slots come first and their receivers are nodes of that patch in non-decreasing order; -1 marks padding; in every draw some patch has all 1024 slots live. `mesh_senders`: A live slot of patch (a, b) sends from a node of patch (a + p, b + q), p and q in -1, 0, 1, with latitude never leaving the range and longitude wrapping round; a padding slot names a node of its own patch. `mesh_receivers`: in each patch's block of 512 slots the live slots come first and their receivers are nodes of that patch in non-decreasing order; -1 marks padding; in every draw some patch has all 512 slots live.
All inputs are finite; a program needn't handle non-finite values.
Results may differ from a plain program's by a relative error of at most 0.0003.
Values sent between devices are 32-bit elements; how exact they have to be, the bound alone decides.
A program may use at most 64 MiB of HBM per device.

v0:
```python
import jax
import jax.numpy as jnp
from jax import lax
from jax.sharding import PartitionSpec as P

RIM = 2


HIGHEST = lax.Precision.HIGHEST
epsilon = 1e-05


def in_blocks(array, dim, count):
    dims = array.shape
    blocks = array.reshape(*dims[:dim], count, dims[dim] // count, *dims[dim + 1 :])
    return jnp.moveaxis(blocks, dim, 0)


def sent_and_summed(array, axis, dim):
    blocks = in_blocks(array, dim, lax.axis_size(axis))
    arrived = lax.all_to_all(blocks, axis, split_axis=0, concat_axis=0, tiled=True)
    return arrived.sum(axis=0)


def copy_for_each(array, axis):
    count = lax.axis_size(axis)
    return lax.all_to_all(
        jnp.broadcast_to(array[None], (count, *array.shape)), axis, 0, 0, tiled=True
    )


def taken_together(array, axis):
    everything = copy_for_each(array, axis)
    return jnp.sum(everything, axis=0)


def packed_total(arrays, axis):
    ends = [0]
    for a in arrays:
        ends.append(ends[-1] + a.size)
    running = taken_together(jnp.concatenate([a.ravel() for a in arrays]), axis)
    return tuple((running[b:e].reshape(a.shape) for a, b, e in zip(arrays, ends, ends[1:])))


def padded_2(block, sides, width):
    for axis, dim in sides:
        count = lax.axis_size(axis)
        forward = [(i, i + 1) for i in range(count - 1)]
        forward.append((count - 1, 0))
        backward = [(target, source) for source, target in forward]
        low = lax.ppermute(
            lax.slice_in_dim(block, block.shape[dim] - width, None, axis=dim), axis, forward
        )
        high = lax.ppermute(lax.slice_in_dim(block, 0, width, axis=dim), axis, backward)
        block = jnp.concatenate([low, block, high], axis=dim)
    return block


def joined_along(blocks, dim):
    dims = list(blocks.shape[1:])
    dims[dim] *= blocks.shape[0]
    return jnp.moveaxis(blocks, 0, dim).reshape(dims)


def gather_directly(array, axis, dim):
    blocks = copy_for_each(array, axis)
    return joined_along(blocks, dim)


def matmul(left, right):
    return jnp.dot(left, right, precision=HIGHEST, preferred_element_type=jnp.float32)


def contract_first(left, right):
    return lax.dot_general(
        left, right, (((0,), (0,)), ((), ())), precision=HIGHEST, preferred_element_type=jnp.float32
    )


def normalise_shares(section_index, partial_value, onehot, out_bias, norm_gain, norm_shift):
    share = sent_and_summed(partial_value, "hid", 1)
    share_width = share.shape[1]
    offset = lax.axis_index("hid") * share_width
    share = share + lax.dynamic_slice_in_dim(out_bias[section_index], offset, share_width)
    totals, squares = packed_total((jnp.sum(share, axis=1), jnp.sum(share * share, axis=1)), "hid")
    full_width = share_width * lax.axis_size("hid")
    center = (totals / full_width)[:, None]
    spread = squares[:, None] / full_width - center * center
    gain_share = lax.dynamic_slice_in_dim(norm_gain[section_index], offset, share_width)
    shift_share = lax.dynamic_slice_in_dim(norm_shift[section_index], offset, share_width)
    normed = (share - center) * lax.rsqrt(spread + epsilon) * gain_share + shift_share
    return contract_first(onehot, normed)


def per_device(
    grid_latent,
    mesh_latent,
    grid_edge_feats,
    grid_senders,
    grid_receivers,
    mesh_edge_feats,
    mesh_senders,
    mesh_receivers,
    edge_weight,
    sender_weight,
    receiver_weight,
    first_bias,
    out_weight,
    out_bias,
    norm_gain,
    norm_shift,
):
    lat_index = lax.axis_index("lat")
    lon_index = lax.axis_index("lon")
    lon_count = lax.axis_size("lon")
    hid_index = lax.axis_index("hid")
    hid_count = lax.axis_size("hid")
    block_rows, block_cols, latent_width = grid_latent.shape
    node_count = mesh_latent.shape[2]
    patch_index = lat_index * lon_count + lon_index
    mesh_own = mesh_latent.reshape(node_count, latent_width)
    node_ids = jnp.arange(node_count, dtype=jnp.int32)

    def aggregate(section_index, send_rows, receivers, receiver_table, feats):
        local_node = receivers.reshape(-1) - patch_index * node_count
        onehot = (local_node[:, None] == node_ids[None, :]).astype(jnp.float32)
        recv_terms = matmul(receiver_table, receiver_weight[section_index])
        recv_rows = jnp.take(recv_terms, jnp.clip(local_node, 0, node_count - 1), axis=0)
        edge_terms = contract_first(feats.reshape(feats.shape[2], -1), edge_weight[section_index])
        hidden = jax.nn.silu(send_rows + recv_rows + edge_terms + first_bias[section_index])
        partial_value = matmul(hidden, out_weight[section_index])
        incoming = normalise_shares(
            section_index, partial_value, onehot, out_bias, norm_gain, norm_shift
        )
        return incoming

    own_terms = matmul(grid_latent.reshape(block_rows * block_cols, latent_width), sender_weight[0])
    own_terms = own_terms.reshape(block_rows, block_cols, own_terms.shape[1])
    padded = padded_2(own_terms, (("lat", 0), ("lon", 1)), RIM)
    grid_table = padded.reshape(-1, own_terms.shape[2])
    total_lon = block_cols * lon_count
    grid_ids = grid_senders.reshape(-1)
    cell_row = grid_ids // total_lon - lat_index * block_rows + RIM
    cell_col = (grid_ids % total_lon - lon_index * block_cols + RIM) % total_lon
    grid_rows = jnp.take(grid_table, cell_row * (block_cols + 2 * RIM) + cell_col, axis=0)
    incoming = aggregate(0, grid_rows, grid_receivers, mesh_own, grid_edge_feats)
    mesh_mid = mesh_own + gather_directly(incoming, "hid", 1)
    own_terms = matmul(mesh_mid, sender_weight[1])
    padded = padded_2(
        own_terms.reshape(1, 1, node_count, own_terms.shape[1]), (("lat", 0), ("lon", 1)), 1
    )
    mesh_table = padded.reshape(-1, own_terms.shape[1])
    mesh_ids = mesh_senders.reshape(-1)
    source_patch = mesh_ids // node_count
    row_offset = source_patch // lon_count - lat_index + 1
    col_offset = (source_patch % lon_count - lon_index + 1) % lon_count
    mesh_rows = jnp.take(
        mesh_table, (row_offset * 3 + col_offset) * node_count + mesh_ids % node_count, axis=0
    )
    incoming = aggregate(1, mesh_rows, mesh_receivers, mesh_mid, mesh_edge_feats)
    share_width = latent_width // hid_count
    mesh_out = (
        lax.dynamic_slice_in_dim(mesh_mid, hid_index * share_width, share_width, 1) + incoming
    )
    return mesh_out.reshape(1, 1, node_count, share_width)


def solution(mesh):
    return jax.shard_map(
        per_device,
        mesh=mesh,
        in_specs=(
            P("lat", "lon", None),
            P("lat", "lon", None, None),
            P("lat", "lon", None, None),
            P("lat", "lon", None),
            P("lat", "lon", None),
            P("lat", "lon", None, None),
            P("lat", "lon", None),
            P("lat", "lon", None),
            P(None, None, "hid"),
            P(None, None, "hid"),
            P(None, None, "hid"),
            P(None, "hid"),
            P(None, "hid", None),
            P(),
            P(),
            P(),
        ),
        out_specs=P("lat", "lon", None, "hid"),
        check_vma=False,
    )
```

profile of v0, /device:TPU:192, one launch (start us, length us, event | category | flops | bytes accessed | tf_op | source)
XLA Modules:
  0.0 183.5 jit_solution(15174335624938380692)
XLA Ops:
  0.0 1.6 copy-done
  1.6 2.7 %fusion.26 = f32[1024,128]{1,0:T(8,128)S(1)} fusion(f32[1024,512]{1,0:T(8,128)S(1)} %bitcast.131, f32[2,512,128]{2,1,0:T(8,128)} %param.25), kind=kOutput, calls=%fused_computation.44 | convolution fusion | flops 805306368 | bytes 2883584 | tf_op jit(solution)/shard_map/dot_general | solution.py:71
  4.3 0.7 fusion.113
  5.0 0.0 collective-permute-start.1
  5.0 0.5 collective-permute-start
  5.5 0.1 compare_select_fusion.1
  5.6 1.8 slice_bitcast_fusion
  7.4 0.6 compare_and_fusion
  8.0 2.2 %fusion.24 = f32[512,128]{1,0:T(8,128)S(1)} fusion(f32[2,512,128]{2,1,0:T(8,128)} %param.26, f32[1,1,512,512]{3,2,1,0:T(8,128)} %param.17), kind=kOutput, calls=%fused_computation.42 | convolution fusion | flops 402653184 | bytes 1572864 | tf_op jit(solution)/shard_map/dot_general | solution.py:71
  10.2 0.0 collective-permute-done.1
  10.3 3.5 %collective-permute-start.2 = (f32[12,2,128]{2,1,0:T(2,128)S(1)}, f32[12,2,128]{2,1,0:T(2,128)S(1)}, u32[]{:S(2)}, u32[]{:S(2)}) collective-permute-start(f32[12,2,128]{2,1,0:T(2,128)S(1)} %get-tuple-element.13), channel_id=1, source_target_pairs={{0,4},{4,8},{8,12},{12,16},{16,20},{20,24},{24,28},{28,0},{1,5},{5... | collective-permute-start | bytes 36872 | tf_op jit(solution)/shard_map/ppermute | solution.py:51
  13.8 3.8 %collective-permute-start.3 = (f32[12,2,128]{2,1,0:T(2,128)S(1)}, f32[12,2,128]{2,1,0:T(2,128)S(1)}, u32[]{:S(2)}, u32[]{:S(2)}) collective-permute-start(f32[12,2,128]{2,1,0:T(2,128)S(1)} %get-tuple-element.14), channel_id=1, source_target_pairs={{4,0},{8,4},{12,8},{16,12},{20,16},{24,20},{28,24},{0,28},{5,1},{9... | collective-permute-start | bytes 36872 | tf_op jit(solution)/shard_map/ppermute | solution.py:54
  17.6 0.8 slice_bitcast_fusion.2
  18.4 0.8 copy.34
  19.2 2.8 %gather_fusion.1 = f32[1024,128]{1,0:T(8,128)S(1)} fusion(f32[512,128]{1,0:T(8,128)S(1)} %fusion.24, s32[1024]{0:T(1024)S(1)} %broadcast_clamp_fusion), kind=kCustom, calls=%fused_computation.1 | custom fusion | bytes 1052672 | tf_op jit(solution)/shard_map/jit(_take)/gather | solution.py:128
  22.0 0.0 collective-permute-done.2
  22.0 0.0 collective-permute-done.3
  22.1 2.0 %pad_maximum_fusion.1 = f32[12,132,128]{2,1,0:T(8,128)} fusion(f32[12,2,128]{2,1,0:T(2,128)S(1)} %collective-permute-done.3, f32[2,128,128]{2,1,0:T(8,128)} %copy-done.6, f32[8,128,128]{2,1,0:T(8,128)S(1)} %bitcast.136, f32[2,128,128]{2,1,0:T(8,128)} %copy-done.7, f32[12,2,128]{2,1,0:T(2,128)S(1)} %collective-permute-done.2), kind=kLoop, calls=%fused_computation.20 | loop fusion | flops 811008 | bytes 1622016 | tf_op jit(solution)/shard_map/concatenate | solution.py:55
  24.0 1.2 reshape.565
  25.2 0.0 copy-start.8
  25.2 0.0 copy-start.12
  25.3 4.0 %gather_fusion = f32[1024,128]{1,0:T(8,128)} fusion(f32[1584,128]{1,0:T(8,128)S(1)} %reshape.565, s32[1024]{0:T(1024)S(1)} %broadcast_clamp_fusion.1), kind=kCustom, calls=%fused_computation | custom fusion | bytes 1052672 | tf_op jit(solution)/shard_map/jit(_take)/gather | solution.py:145
  29.3 2.5 %fusion.1 = f32[1024,128]{1,0:T(8,128)S(1)} fusion(f32[1024,128]{1,0:T(8,128)S(1)} %gather_fusion.1, f32[1024,128]{1,0:T(8,128)} %gather_fusion, f32[128]{0:T(128)S(1)} %get-tuple-element.30, pred[1024]{0:T(1024)(128)(4,1)S(1)} %get-tuple-element.32, pred[1024]{0:T(1024)(128)(4,1)S(1)} %copy-done.17, f32[1,1,4,1024]{3,2,1,0:T(4,128)S(1)} %copy-done.8, ...), kind=kOutput, calls=%fused_computation.10 | convolution fusion | flops 6946816 | bytes 1593856 | tf_op jit(solution)/shard_map/dot_general | solution.py:75
  31.8 4.1 %convolution_bitcast_fusion = f32[4,1024,128]{2,1,0:T(8,128)} fusion(f32[4,128,128]{2,1,0:T(8,128)} %bitcast.139, f32[1024,128]{1,0:T(8,128)S(1)} %fusion.1), kind=kOutput, calls=%fused_computation.7 | convolution fusion | flops 805830656 | bytes 2883584 | tf_op jit(solution)/shard_map/dot_general | solution.py:71
  35.9 4.6 %all-to-all-start = ((f32[4,1024,128]{2,1,0:T(8,128)}), f32[4,1024,128]{2,1,0:T(8,128)}, u32[]{:S(2)}, u32[]{:S(2)}) async-start(f32[4,1024,128]{2,1,0:T(8,128)} %convolution_bitcast_fusion), calls=%async_computation | async-start | bytes 4194304 | tf_op jit(solution)/shard_map/all_to_all | solution.py:21
  40.6 25.7 %all-to-all-done = f32[4,1024,128]{2,1,0:T(8,128)} async-done(((f32[4,1024,128]{2,1,0:T(8,128)}), f32[4,1024,128]{2,1,0:T(8,128)}, u32[]{:S(2)}, u32[]{:S(2)}) %all-to-all-start) | async-done | bytes 2097184 | tf_op jit(solution)/shard_map/all_to_all | solution.py:21
  66.3 1.8 reduce_sum.72
  68.1 0.3 add_reduce_fusion
  68.4 0.6 broadcast_in_dim.45
  69.0 3.3 %all-to-all-start.1 = ((f32[4,1,2048]{2,1,0:T(1,128)}), f32[4,1,2048]{2,1,0:T(1,128)S(1)}, u32[]{:S(2)}, u32[]{:S(2)}) async-start(f32[4,1,2048]{2,1,0:T(1,128)} %broadcast_in_dim.45), calls=%async_computation.1 | async-start | bytes 65536 | tf_op jit(solution)/shard_map/all_to_all | solution.py:27
  72.3 5.4 %all-to-all-done.1 = f32[4,1,2048]{2,1,0:T(1,128)S(1)} async-done(((f32[4,1,2048]{2,1,0:T(1,128)}), f32[4,1,2048]{2,1,0:T(1,128)S(1)}, u32[]{:S(2)}, u32[]{:S(2)}) %all-to-all-start.1) | async-done | bytes 32800 | tf_op jit(solution)/shard_map/all_to_all | solution.py:27
  77.8 2.2 %fusion = f32[512,128]{1,0:T(8,128)S(1)} fusion(s32[1024]{0:T(1024)S(1)} %bitcast.145, f32[1024,128]{1,0:T(8,128)S(1)} %reduce_sum.72, f32[128]{0:T(128)S(1)} %fusion.105, f32[128]{0:T(128)S(1)} %get-tuple-element.35, f32[1024]{0:T(1024)S(1)} %get-tuple-element.20, f32[1024]{0:T(1024)S(1)} %get-tuple-element.19, f32[128]{0:T(128)S(1)} %get-tuple-element.34), kind=kOutput, calls=%fused_computation.6 | convolution fusion | flops 806486016 | bytes 800256 | tf_op jit(solution)/shard_map/dot_general | solution.py:75
  80.0 1.1 broadcast_in_dim.46
  81.1 3.8 %all-to-all-start.2 = ((f32[4,512,128]{2,1,0:T(8,128)}), f32[4,512,128]{2,1,0:T(8,128)S(1)}, u32[]{:S(2)}, u32[]{:S(2)}) async-start(f32[4,512,128]{2,1,0:T(8,128)} %broadcast_in_dim.46), calls=%async_computation.2 | async-start | bytes 2097152 | tf_op jit(solution)/shard_map/all_to_all | solution.py:27
  84.9 2.6 %copy.38 = f32[1,1,512,512]{2,3,1,0:T(8,128)} copy(f32[1,1,512,512]{3,2,1,0:T(8,128)} %param.17) | data formatting | bytes 2097152 | tf_op args[1]
  87.5 0.1 compare_select_fusion.4
  87.5 13.4 %all-to-all-done.2 = f32[4,512,128]{2,1,0:T(8,128)S(1)} async-done(((f32[4,512,128]{2,1,0:T(8,128)}), f32[4,512,128]{2,1,0:T(8,128)S(1)}, u32[]{:S(2)}, u32[]{:S(2)}) %all-to-all-start.2) | async-done | bytes 1048608 | tf_op jit(solution)/shard_map/all_to_all | solution.py:27
  100.9 1.3 copy.36
  102.2 3.4 %convolution_bitcast_fusion.2 = f32[1,1,512,128]{3,2,1,0:T(8,128)S(1)} fusion(f32[1,1,512,512]{2,3,1,0:T(8,128)} %copy.38, f32[1,1,512,512]{2,3,1,0:T(8,128)} %bitcast.132, f32[2,512,128]{2,1,0:T(8,128)} %param.25), kind=kOutput, calls=%fused_computation.13 | convolution fusion | flops 402915328 | bytes 2621440 | tf_op jit(solution)/shard_map/dot_general | solution.py:71
  105.7 0.0 collective-permute-start.5
  105.7 0.5 collective-permute-start.4
  106.2 3.3 %collective-permute-done.5 = f32[1,1,512,128]{3,2,1,0:T(8,128)S(1)} collective-permute-done((f32[1,1,512,128]{3,2,1,0:T(8,128)S(1)}, f32[1,1,512,128]{3,2,1,0:T(8,128)S(1)}, u32[]{:S(2)}, u32[]{:S(2)}) %collective-permute-start.5) | collective-permute-done | bytes 262176 | tf_op jit(solution)/shard_map/ppermute | solution.py:54
  109.6 1.9 %collective-permute-done.4 = f32[1,1,512,128]{3,2,1,0:T(8,128)S(1)} collective-permute-done((f32[1,1,512,128]{3,2,1,0:T(8,128)S(1)}, f32[1,1,512,128]{3,2,1,0:T(8,128)S(1)}, u32[]{:S(2)}, u32[]{:S(2)}) %collective-permute-start.4) | collective-permute-done | bytes 262176 | tf_op jit(solution)/shard_map/ppermute | solution.py:51
  111.5 1.0 pad_maximum_fusion.2
  112.5 3.9 %collective-permute-start.7 = (f32[3,1,512,128]{3,2,1,0:T(8,128)}, f32[3,1,512,128]{3,2,1,0:T(8,128)}, u32[]{:S(2)}, u32[]{:S(2)}) collective-permute-start(f32[3,1,512,128]{3,2,1,0:T(8,128)} %pad_maximum_fusion.2), channel_id=1, source_target_pairs={{4,0},{8,4},{12,8},{16,12},{20,16},{24,20},{28,24},{0,28},{5,1},{9... | collective-permute-start | bytes 2359304 | tf_op jit(solution)/shard_map/ppermute | solution.py:54
  116.5 1.9 %collective-permute-start.6 = (f32[3,1,512,128]{3,2,1,0:T(8,128)}, f32[3,1,512,128]{3,2,1,0:T(8,128)}, u32[]{:S(2)}, u32[]{:S(2)}) collective-permute-start(f32[3,1,512,128]{3,2,1,0:T(8,128)} %pad_maximum_fusion.2), channel_id=1, source_target_pairs={{0,4},{4,8},{8,12},{12,16},{16,20},{20,24},{24,28},{28,0},{1,5},{5... | collective-permute-start | bytes 2359304 | tf_op jit(solution)/shard_map/ppermute | solution.py:51
  118.4 0.8 copy.39
  119.3 1.3 fusion.64
  120.6 3.4 %fusion.3 = f32[512,128]{1,0:T(8,128)S(1)} fusion(f32[1,1,512,512]{2,3,1,0:T(8,128)} %copy.38, f32[1,1,512,512]{2,3,1,0:T(8,128)} %bitcast.133, f32[2,512,128]{2,1,0:T(8,128)} %param.26), kind=kOutput, calls=%fused_computation.15 | convolution fusion | flops 402915328 | bytes 2621440 | tf_op jit(solution)/shard_map/dot_general | solution.py:71
  124.0 1.6 gather_fusion.3
  125.6 9.0 %collective-permute-done.7 = f32[3,1,512,128]{3,2,1,0:T(8,128)} collective-permute-done((f32[3,1,512,128]{3,2,1,0:T(8,128)}, f32[3,1,512,128]{3,2,1,0:T(8,128)}, u32[]{:S(2)}, u32[]{:S(2)}) %collective-permute-start.7) | collective-permute-done | bytes 786464 | tf_op jit(solution)/shard_map/ppermute | solution.py:54
  134.6 5.6 %collective-permute-done.6 = f32[3,1,512,128]{3,2,1,0:T(8,128)} collective-permute-done((f32[3,1,512,128]{3,2,1,0:T(8,128)}, f32[3,1,512,128]{3,2,1,0:T(8,128)}, u32[]{:S(2)}, u32[]{:S(2)}) %collective-permute-start.6) | collective-permute-done | bytes 786464 | tf_op jit(solution)/shard_map/ppermute | solution.py:51
  140.1 3.2 %pad_maximum_fusion = f32[3,3,512,128]{3,2,1,0:T(8,128)} fusion(f32[3,1,512,128]{3,2,1,0:T(8,128)} %collective-permute-done.7, f32[1,1,512,128]{3,2,1,0:T(8,128)} %copy-done.3, f32[1,1,512,128]{3,2,1,0:T(8,128)} %copy-done.1, f32[1,1,512,128]{3,2,1,0:T(8,128)} %copy-done.4, f32[3,1,512,128]{3,2,1,0:T(8,128)} %collective-permute-done.6), kind=kLoop, calls=%fused_computation.4 | loop fusion | flops 2359296 | bytes 4718592 | tf_op jit(solution)/shard_map/concatenate | solution.py:55
  143.4 3.3 %gather_fusion.2 = f32[512,128]{1,0:T(8,128)} fusion(f32[4608,128]{1,0:T(8,128)} %bitcast.134, s32[1024]{0:T(1024)S(1)} %pad_clamp_fusion.1), kind=kCustom, calls=%fused_computation.2 | custom fusion | bytes 526336 | tf_op jit(solution)/shard_map/jit(_take)/gather | solution.py:157
  146.7 3.2 %convolution_bitcast_fusion.1 = f32[4,512,128]{2,1,0:T(8,128)} fusion(f32[4,128,128]{2,1,0:T(8,128)S(1)} %bitcast.138, f32[512,128]{1,0:T(8,128)} %fusion.64, f32[512,128]{1,0:T(8,128)} %gather_fusion.3, f32[512,128]{1,0:T(8,128)} %gather_fusion.2, f32[128]{0:T(128)S(1)} %get-tuple-element.29, pred[512]{0:T(512)(128)(4,1)S(1)} %compare_and_fusion.2, ...), kind=kOutput, calls=%fused_computation.8 | convolution fusion | flops 403243008 | bytes 2098688 | tf_op jit(solution)/shard_map/dot_general | solution.py:71
  149.9 4.3 %all-to-all-start.3 = ((f32[4,512,128]{2,1,0:T(8,128)}), f32[4,512,128]{2,1,0:T(8,128)}, u32[]{:S(2)}, u32[]{:S(2)}) async-start(f32[4,512,128]{2,1,0:T(8,128)} %convolution_bitcast_fusion.1), calls=%async_computation.3 | async-start | bytes 2097152 | tf_op jit(solution)/shard_map/all_to_all | solution.py:21
  154.2 15.5 %all-to-all-done.3 = f32[4,512,128]{2,1,0:T(8,128)} async-done(((f32[4,512,128]{2,1,0:T(8,128)}), f32[4,512,128]{2,1,0:T(8,128)}, u32[]{:S(2)}, u32[]{:S(2)}) %all-to-all-start.3) | async-done | bytes 1048608 | tf_op jit(solution)/shard_map/all_to_all | solution.py:21
  169.7 1.3 reduce_sum.76
  171.0 0.2 add_reduce_fusion.1
  171.3 0.6 broadcast_in_dim.76
  171.9 3.3 %all-to-all-start.4 = ((f32[4,1,1024]{2,1,0:T(1,128)}), f32[4,1,1024]{2,1,0:T(1,128)S(1)}, u32[]{:S(2)}, u32[]{:S(2)}) async-start(f32[4,1,1024]{2,1,0:T(1,128)} %broadcast_in_dim.76), calls=%async_computation.4 | async-start | bytes 32768 | tf_op jit(solution)/shard_map/all_to_all | solution.py:27
  175.2 1.1 copy_bitcast_fusion
  176.3 4.2 %all-to-all-done.4 = f32[4,1,1024]{2,1,0:T(1,128)S(1)} async-done(((f32[4,1,1024]{2,1,0:T(1,128)}), f32[4,1,1024]{2,1,0:T(1,128)S(1)}, u32[]{:S(2)}, u32[]{:S(2)}) %all-to-all-start.4) | async-done | bytes 16416 | tf_op jit(solution)/shard_map/all_to_all | solution.py:27
  180.5 3.0 %fusion.2 = f32[1,1,512,128]{3,2,1,0:T(8,128)} fusion(s32[512]{0:T(512)S(1)} %bitcast.142, f32[512,512]{1,0:T(8,128)} %copy_bitcast_fusion, s32[]{:T(128)S(6)} %select_n.223, f32[512,512]{1,0:T(8,128)} %bitcast.137, f32[512,128]{1,0:T(8,128)S(1)} %reduce_sum.76, f32[128]{0:T(128)S(1)} %get-tuple-element.37, f32[128]{0:T(128)S(1)} %get-tuple-element.36, ...), kind=kOutput, calls=%fused_computation.12 | convolution fusion | flops 403374080 | bytes 1056260 | tf_op jit(solution)/shard_map/dot_general | solution.py:75
  (57 shorter events, 0.3 us)
Async XLA Ops:
  0.0 1.6 copy-start
  0.0 5.5 %copy-start.9 = (s32[1,1,1024]{2,1,0:T(1,128)S(1)}, s32[1,1,1024]{2,1,0:T(1,128)}, u32[]{:S(2)}) copy-start(s32[1,1,1024]{2,1,0:T(1,128)} %param.19) | copy-start | bytes 12292
  0.0 7.4 %copy-start.13 = (s32[1,1,1024]{2,1,0:T(1,128)S(1)}, s32[1,1,1024]{2,1,0:T(1,128)}, u32[]{:S(2)}) copy-start(s32[1,1,1024]{2,1,0:T(1,128)} %param.20) | copy-start | bytes 12292
  5.0 5.2 %collective-permute-start.1 = (f32[2,128,128]{2,1,0:T(8,128)}, f32[2,128,128]{2,1,0:T(8,128)S(1)}, u32[]{:S(2)}, u32[]{:S(2)}) collective-permute-start(f32[2,128,128]{2,1,0:T(8,128)} %bitcast.7), channel_id=1, source_target_pairs={{32,0},{64,32},{96,64},{128,96},{160,128},{192,160},{224,192},{256... | collective-permute-start | bytes 393224 | tf_op jit(solution)/shard_map/ppermute | solution.py:54
  5.0 5.3 %collective-permute-start = (f32[2,128,128]{2,1,0:T(8,128)S(1)}, f32[2,128,128]{2,1,0:T(8,128)S(1)}, u32[]{:S(2)}, u32[]{:S(2)}) collective-permute-start(f32[2,128,128]{2,1,0:T(8,128)S(1)} %bitcast.140), channel_id=1, source_target_pairs={{0,32},{32,64},{64,96},{96,128},{128,160},{160,192},{192,224},{224... | collective-permute-start | bytes 393224 | tf_op jit(solution)/shard_map/ppermute | solution.py:51
  10.3 8.1 %copy-start.6 = (f32[2,128,128]{2,1,0:T(8,128)}, f32[2,128,128]{2,1,0:T(8,128)S(1)}, u32[]{:S(2)}) copy-start(f32[2,128,128]{2,1,0:T(8,128)S(1)} %collective-permute-done.1) | copy-start | bytes 393220
  10.3 8.1 %copy-start.7 = (f32[2,128,128]{2,1,0:T(8,128)}, f32[2,128,128]{2,1,0:T(8,128)S(1)}, u32[]{:S(2)}) copy-start(f32[2,128,128]{2,1,0:T(8,128)S(1)} %collective-permute-done) | copy-start | bytes 393220
  10.3 11.7 %collective-permute-start.2 = (f32[12,2,128]{2,1,0:T(2,128)S(1)}, f32[12,2,128]{2,1,0:T(2,128)S(1)}, u32[]{:S(2)}, u32[]{:S(2)}) collective-permute-start(f32[12,2,128]{2,1,0:T(2,128)S(1)} %get-tuple-element.13), channel_id=1, source_target_pairs={{0,4},{4,8},{8,12},{12,16},{16,20},{20,24},{24,28},{28,0},{1,5},{5... | collective-permute-start | bytes 36872 | tf_op jit(solution)/shard_map/ppermute | solution.py:51
  13.8 8.3 %collective-permute-start.3 = (f32[12,2,128]{2,1,0:T(2,128)S(1)}, f32[12,2,128]{2,1,0:T(2,128)S(1)}, u32[]{:S(2)}, u32[]{:S(2)}) collective-permute-start(f32[12,2,128]{2,1,0:T(2,128)S(1)} %get-tuple-element.14), channel_id=1, source_target_pairs={{4,0},{8,4},{12,8},{16,12},{20,16},{24,20},{28,24},{0,28},{5,1},{9... | collective-permute-start | bytes 36872 | tf_op jit(solution)/shard_map/ppermute | solution.py:54
  25.2 4.1 %copy-start.8 = (f32[1,1,4,1024]{3,2,1,0:T(4,128)S(1)}, f32[1,1,4,1024]{3,2,1,0:T(4,128)}, u32[]{:S(2)}) copy-start(f32[1,1,4,1024]{3,2,1,0:T(4,128)} %param.18) | copy-start | bytes 49156
  25.2 4.0 %copy-start.12 = (f32[2,4,128]{2,1,0:T(4,128)S(1)}, f32[2,4,128]{2,1,0:T(4,128)}, u32[]{:S(2)}) copy-start(f32[2,4,128]{2,1,0:T(4,128)} %param.24) | copy-start | bytes 12292
  25.3 4.0 %copy-start.17 = (pred[1024]{0:T(1024)(128)(4,1)S(1)}, pred[1024]{0:T(1024)(128)(4,1)}, u32[]{:S(2)}) copy-start(pred[1024]{0:T(1024)(128)(4,1)} %get-tuple-element.33) | copy-start | bytes 3076
  35.9 4.6 %copy-start.14 = (f32[2,512]{1,0:T(2,128)S(1)}, f32[2,512]{1,0:T(2,128)}, u32[]{:S(2)}) copy-start(f32[2,512]{1,0:T(2,128)} %param.29) | copy-start | bytes 12292
  35.9 4.6 %copy-start.15 = (f32[2,512]{1,0:T(2,128)S(1)}, f32[2,512]{1,0:T(2,128)}, u32[]{:S(2)}) copy-start(f32[2,512]{1,0:T(2,128)} %param.30) | copy-start | bytes 12292
  35.9 4.7 %copy-start.16 = (f32[2,512]{1,0:T(2,128)S(1)}, f32[2,512]{1,0:T(2,128)}, u32[]{:S(2)}) copy-start(f32[2,512]{1,0:T(2,128)} %param.31) | copy-start | bytes 12292
  35.9 30.4 %all-to-all-start = ((f32[4,1024,128]{2,1,0:T(8,128)}), f32[4,1024,128]{2,1,0:T(8,128)}, u32[]{:S(2)}, u32[]{:S(2)}) async-start(f32[4,1024,128]{2,1,0:T(8,128)} %convolution_bitcast_fusion), calls=%async_computation | async-start | bytes 4194304 | tf_op jit(solution)/shard_map/all_to_all | solution.py:21
  69.0 8.7 %all-to-all-start.1 = ((f32[4,1,2048]{2,1,0:T(1,128)}), f32[4,1,2048]{2,1,0:T(1,128)S(1)}, u32[]{:S(2)}, u32[]{:S(2)}) async-start(f32[4,1,2048]{2,1,0:T(1,128)} %broadcast_in_dim.45), calls=%async_computation.1 | async-start | bytes 65536 | tf_op jit(solution)/shard_map/all_to_all | solution.py:27
  81.1 6.4 %copy-start.11 = (s32[1,1,512]{2,1,0:T(1,128)S(1)}, s32[1,1,512]{2,1,0:T(1,128)}, u32[]{:S(2)}) copy-start(s32[1,1,512]{2,1,0:T(1,128)} %param.22) | copy-start | bytes 6148
  81.1 6.4 %copy-start.18 = (s32[1,1,512]{2,1,0:T(1,128)S(1)}, s32[1,1,512]{2,1,0:T(1,128)}, u32[]{:S(2)}) copy-start(s32[1,1,512]{2,1,0:T(1,128)} %param.23) | copy-start | bytes 6148
  81.1 19.8 %all-to-all-start.2 = ((f32[4,512,128]{2,1,0:T(8,128)}), f32[4,512,128]{2,1,0:T(8,128)S(1)}, u32[]{:S(2)}, u32[]{:S(2)}) async-start(f32[4,512,128]{2,1,0:T(8,128)} %broadcast_in_dim.46), calls=%async_computation.2 | async-start | bytes 2097152 | tf_op jit(solution)/shard_map/all_to_all | solution.py:27
  102.2 16.2 %copy-start.5 = (f32[512,128]{0,1:T(8,128)S(1)}, f32[512,128]{0,1:T(8,128)}, u32[]{:S(2)}) copy-start(f32[512,128]{0,1:T(8,128)} %get-tuple-element.15) | copy-start | bytes 786436
  102.2 17.1 %copy-start.10 = (f32[1,1,4,512]{3,2,1,0:T(4,128)S(1)}, f32[1,1,4,512]{3,2,1,0:T(4,128)}, u32[]{:S(2)}) copy-start(f32[1,1,4,512]{3,2,1,0:T(4,128)} %param.21) | copy-start | bytes 24580
  105.7 5.8 %copy-start.1 = (f32[1,1,512,128]{3,2,1,0:T(8,128)}, f32[1,1,512,128]{3,2,1,0:T(8,128)S(1)}, u32[]{:S(2)}) copy-start(f32[1,1,512,128]{3,2,1,0:T(8,128)S(1)} %convolution_bitcast_fusion.2) | copy-start | bytes 786436
  105.7 3.9 %collective-permute-start.5 = (f32[1,1,512,128]{3,2,1,0:T(8,128)S(1)}, f32[1,1,512,128]{3,2,1,0:T(8,128)S(1)}, u32[]{:S(2)}, u32[]{:S(2)}) collective-permute-start(f32[1,1,512,128]{3,2,1,0:T(8,128)S(1)} %convolution_bitcast_fusion.2), channel_id=1, source_target_pairs={{32,0},{64,32},{96,64},{128,96},{160,128},{192,160},{224,192},{256... | collective-permute-start | bytes 786440 | tf_op jit(solution)/shard_map/ppermute | solution.py:54
  105.7 5.8 %collective-permute-start.4 = (f32[1,1,512,128]{3,2,1,0:T(8,128)S(1)}, f32[1,1,512,128]{3,2,1,0:T(8,128)S(1)}, u32[]{:S(2)}, u32[]{:S(2)}) collective-permute-start(f32[1,1,512,128]{3,2,1,0:T(8,128)S(1)} %convolution_bitcast_fusion.2), channel_id=1, source_target_pairs={{0,32},{32,64},{64,96},{96,128},{128,160},{160,192},{192,224},{224... | collective-permute-start | bytes 786440 | tf_op jit(solution)/shard_map/ppermute | solution.py:51
  109.6 2.9 %copy-start.3 = (f32[1,1,512,128]{3,2,1,0:T(8,128)}, f32[1,1,512,128]{3,2,1,0:T(8,128)S(1)}, u32[]{:S(2)}) copy-start(f32[1,1,512,128]{3,2,1,0:T(8,128)S(1)} %collective-permute-done.5) | copy-start | bytes 786436
  111.5 5.0 %copy-start.4 = (f32[1,1,512,128]{3,2,1,0:T(8,128)}, f32[1,1,512,128]{3,2,1,0:T(8,128)S(1)}, u32[]{:S(2)}) copy-start(f32[1,1,512,128]{3,2,1,0:T(8,128)S(1)} %collective-permute-done.4) | copy-start | bytes 786436
  112.5 22.1 %collective-permute-start.7 = (f32[3,1,512,128]{3,2,1,0:T(8,128)}, f32[3,1,512,128]{3,2,1,0:T(8,128)}, u32[]{:S(2)}, u32[]{:S(2)}) collective-permute-start(f32[3,1,512,128]{3,2,1,0:T(8,128)} %pad_maximum_fusion.2), channel_id=1, source_target_pairs={{4,0},{8,4},{12,8},{16,12},{20,16},{24,20},{28,24},{0,28},{5,1},{9... | collective-permute-start | bytes 2359304 | tf_op jit(solution)/shard_map/ppermute | solution.py:54
  116.5 23.7 %collective-permute-start.6 = (f32[3,1,512,128]{3,2,1,0:T(8,128)}, f32[3,1,512,128]{3,2,1,0:T(8,128)}, u32[]{:S(2)}, u32[]{:S(2)}) collective-permute-start(f32[3,1,512,128]{3,2,1,0:T(8,128)} %pad_maximum_fusion.2), channel_id=1, source_target_pairs={{0,4},{4,8},{8,12},{12,16},{16,20},{20,24},{24,28},{28,0},{1,5},{5... | collective-permute-start | bytes 2359304 | tf_op jit(solution)/shard_map/ppermute | solution.py:51
  143.4 3.4 %copy-start.2 = (f32[512,128]{1,0:T(8,128)S(1)}, f32[512,128]{1,0:T(8,128)}, u32[]{:S(2)}) copy-start(f32[512,128]{1,0:T(8,128)} %copy.39) | copy-start | bytes 786436
  149.9 19.8 %all-to-all-start.3 = ((f32[4,512,128]{2,1,0:T(8,128)}), f32[4,512,128]{2,1,0:T(8,128)}, u32[]{:S(2)}, u32[]{:S(2)}) async-start(f32[4,512,128]{2,1,0:T(8,128)} %convolution_bitcast_fusion.1), calls=%async_computation.3 | async-start | bytes 2097152 | tf_op jit(solution)/shard_map/all_to_all | solution.py:21
  171.9 8.6 %all-to-all-start.4 = ((f32[4,1,1024]{2,1,0:T(1,128)}), f32[4,1,1024]{2,1,0:T(1,128)S(1)}, u32[]{:S(2)}, u32[]{:S(2)}) async-start(f32[4,1,1024]{2,1,0:T(1,128)} %broadcast_in_dim.76), calls=%async_computation.4 | async-start | bytes 32768 | tf_op jit(solution)/shard_map/all_to_all | solution.py:27
where the time goes:
time: 185 us; the launch traced here: 183 us
  waiting for transfers between devices  84 us (45%)
  starting transfers between devices  33.4 us (18%)
  matrix products  28.1 us (15%)
  local copies, waits for them, and re-layouts  26.9 us (15%)
  other arithmetic  10.7 us (6%)
    all_to_all x2, waiting for transfers between devices, sent_and_summed(): lax.all_to_all(blocks, axis, split_axis=0, concat_axis=0, tiled=True)  41.2 us
    all_to_all x3, waiting for transfers between devices, copy_for_each(): lax.all_to_all(jnp.broadcast_to(array[None], (count, *array.shape)), axis...  23 us
    dot_general x6, matrix products, matmul(): jnp.dot(left, right, precision=HIGHEST, preferred_element_type=jnp.float32)  19.1 us
    ppermute x4, waiting for transfers between devices, padded_2(): lax.ppermute(lax.slice_in_dim(block, 0, width, axis=dim), axis, backward)  12.3 us
    all_to_all x3, starting transfers between devices, copy_for_each(): lax.all_to_all(jnp.broadcast_to(array[None], (count, *array.shape)), axis...  10.3 us
    dot_general x4, matrix products, contract_first(): lax.dot_general(left, right, (((0,), (0,)), ((), ())), precision=HIGHEST,...  8.99 us
    all_to_all x2, starting transfers between devices, sent_and_summed(): lax.all_to_all(blocks, axis, split_axis=0, concat_axis=0, tiled=True)  8.85 us
    ppermute x4, starting transfers between devices, padded_2(): lax.ppermute(lax.slice_in_dim(block, 0, width, axis=dim), axis, backward)  7.77 us
  transfers between devices with their start and end apart: 13, of which 9 were waited for; matrix products, arithmetic and copies ran while one was open for 11% of the time, Pallas kernels for 0%

commit v1 on v0

v1 whole, which is shorter than its diff:
```python
import jax
import jax.numpy as jnp
from jax import lax
from jax.experimental import pallas as pl
from jax.experimental.pallas import tpu as pltpu
from jax.sharding import PartitionSpec as P

MESH = pl.DeviceIdType.MESH
F32 = jnp.float32
BF16 = jnp.bfloat16
EPS = 1e-05
NLAT, NLON, NHID = 16, 8, 4
C = 512
NODES = 512
GROWS, GCOLS = 8, 128
E1, E2 = 1024, 512
Q2 = E2 // NHID
TABLE = 12 * GCOLS + 96
LEFT = 12 * GCOLS
RIGHT = LEFT + 48
RW, SW, OW = 0, 1, 2


def split(x):
    hi = x.astype(BF16)
    return hi, (x - hi.astype(F32)).astype(BF16)


def dot(a, b):
    return jnp.dot(a, b, preferred_element_type=F32)


def thrice(x):
    hi, lo = split(x)
    return jnp.concatenate([hi, hi, lo], axis=1)


def silu(t):
    return t / (1.0 + jnp.exp(-t))


def layer_norm(m, gain, shift):
    center = jnp.mean(m, axis=1, keepdims=True)
    d = m - center
    spread = jnp.mean(d * d, axis=1, keepdims=True)
    return d * lax.rsqrt(spread + EPS) * gain + shift


def kernel(
    gl, ml, gef, gs, gr, mef, ms, mr, ew, sw, rw, fb, ow, ob, ng, ns,
    out,
    table, mid, xs, idx_v, idx_s, wcol, wout, w3, r2, sel, agg, nrm, ewb, fbb, epack, wpack,
    req, gbuf, rlat, ry, n1, rm, midb,
    load_sem, wx_s, wx_r, wy_s, wy_r, wc_s, wc_r, hx_s, hx_r, q_s, q_r, gl_s, gl_r, gy_s, gy_r,
    a_s, a_r,
):
    a = lax.axis_index("lat")
    b = lax.axis_index("lon")
    h = lax.axis_index("hid")
    core = lax.rem(a, 2)
    ypar = lax.rem(b, 2)
    sib = a + 1 - 2 * core
    zlat = lax.rem(a + NLAT - 1 + 2 * core, NLAT)
    lats = (zlat, sib, a)
    lons = (lax.rem(b + NLON - 1, NLON), b, lax.rem(b + 1, NLON))
    peers = [lax.rem(h + d, NHID) for d in (1, 2, 3)]
    patch = a * NLON + b

    def dev(group, q):
        return (lats[group], lons[q + 1], h)

    around = [(g, q) for g in range(3) for q in (-1, 0, 1) if not (g == 2 and q == 0)]

    barrier = pltpu.get_barrier_semaphore()
    for p in peers:
        pl.semaphore_signal(barrier, inc=1, device_id=(a, b, p), device_id_type=MESH)
    for g, q in around:
        pl.semaphore_signal(barrier, inc=1, device_id=dev(g, q), device_id_type=MESH)

    sent = []

    def send(src, dst, ssem, rsem, device):
        copy = pltpu.make_async_remote_copy(
            src_ref=src, dst_ref=dst, send_sem=ssem, recv_sem=rsem,
            device_id=device, device_id_type=MESH,
        )
        copy.start()
        sent.append(copy)

    def arrived(dst, rsem, device):
        pltpu.make_async_remote_copy(
            src_ref=dst, dst_ref=dst, send_sem=rsem, recv_sem=rsem,
            device_id=device, device_id_type=MESH,
        ).wait_recv()

    own_rows = table.at[pl.ds(2 * GCOLS, GROWS * GCOLS)]
    load_grid = pltpu.make_async_copy(gl, own_rows, load_sem.at[0])
    load_mesh = pltpu.make_async_copy(ml.at[0, 0], mid, load_sem.at[1])
    load_grid.start()
    load_mesh.start()
    own_loads = []
    for s in range(2):
        for i, (src, dst) in enumerate(
            ((rw.at[s], wcol.at[s, RW, h]), (sw.at[s], wcol.at[s, SW, h]), (ow.at[s], wout.at[s, h]))
        ):
            copy = pltpu.make_async_copy(src, dst, load_sem.at[2 + s * 3 + i])
            copy.start()
            own_loads.append(copy)

    ids = gs[0]
    lrow = lax.shift_right_logical(ids, 10) - a * GROWS + 2
    lcol = (lax.bitwise_and(ids, 1023) - b * GCOLS + 2 + 1024) & 1023
    side = (lrow + 6) * 2
    where = jnp.where(
        lcol < 2,
        LEFT + side + lcol,
        jnp.where(lcol >= GCOLS + 2, RIGHT + side + lcol - (GCOLS + 2), lrow * GCOLS + lcol - 2),
    )
    idx_v[...] = jnp.clip(where, 0, TABLE - 1)
    to_smem = pltpu.make_async_copy(idx_v, idx_s, load_sem.at[8])
    to_smem.start()

    pl.semaphore_wait(barrier, 11)

    low = table.at[pl.ds(0, 2 * GCOLS)]
    high = table.at[pl.ds(10 * GCOLS, 2 * GCOLS)]
    top = gl.at[pl.ds(6 * GCOLS, 2 * GCOLS)]
    bottom = gl.at[pl.ds(0, 2 * GCOLS)]
    up = lax.rem(a + 1, NLAT)
    down = lax.rem(a + NLAT - 1, NLAT)
    send(top, low, hx_s.at[0], hx_r.at[0], (up, b, h))
    send(bottom, high, hx_s.at[1], hx_r.at[1], (down, b, h))

    def src_of(s, m):
        return (rw, sw, ow)[m].at[s]

    def dst_of(s, m, who):
        return wout.at[s, who] if m == OW else wcol.at[s, m, who]

    def size_of(m):
        return 32 if m == OW else 128

    def piece(ref, m, which):
        n = size_of(m)
        return ref.at[pl.ds(pl.multiple_of(which * n, n), n)]

    def half(ref, m, which, part):
        n = size_of(m) // 2
        return ref.at[pl.ds(pl.multiple_of(which * 2 * n + part * n, n), n)]

    mine = 2 * core + ypar
    other = 2 * core + 1 - ypar
    sib_mine = 2 * (1 - core) + ypar
    sib_other = 2 * (1 - core) + 1 - ypar

    def x_send(s, m):
        for i, p in enumerate(peers):
            send(
                piece(src_of(s, m), m, mine), piece(dst_of(s, m, h), m, mine),
                wx_s.at[s, m, i], wx_r.at[s, m, i], (a, b, p),
            )

    def x_forward(s, m):
        for i in range(3):
            owner = peers[2 - i]
            arrived(piece(dst_of(s, m, owner), m, mine), wx_r.at[s, m, i], (a, b, owner))
            for part, q in ((0, 1), (1, -1)):
                view = half(dst_of(s, m, owner), m, mine, part)
                send(view, view, wy_s.at[s, m, i, part], wy_r.at[s, m, i, part], dev(2, q))
            view = piece(dst_of(s, m, owner), m, mine)
            send(view, view, wc_s.at[s, m, i, 0], wc_r.at[s, m, i, 0], dev(1, 0))

    def y_forward(s, m):
        for i in range(3):
            owner = peers[2 - i]
            for part, q in ((0, -1), (1, 1)):
                arrived(half(dst_of(s, m, owner), m, other, part), wy_r.at[s, m, i, part], dev(2, q))
            view = piece(dst_of(s, m, owner), m, other)
            send(view, view, wc_s.at[s, m, i, 1], wc_r.at[s, m, i, 1], dev(1, 0))

    def c_wait(s, m):
        for i in range(3):
            owner = peers[2 - i]
            arrived(piece(dst_of(s, m, owner), m, sib_mine), wc_r.at[s, m, i, 0], dev(1, 0))
            arrived(piece(dst_of(s, m, owner), m, sib_other), wc_r.at[s, m, i, 1], dev(1, 0))

    def build(s, m):
        own_loads[s * 3 + m].wait()
        for k in range(NHID):
            block = wout[s, k] if m == OW else wcol[s, m, k]
            hi, lo = split(block)
            if m == OW:
                for t, v in enumerate((hi, lo, hi)):
                    w3[s, m, pl.ds(t * 512 + k * 128, 128), :] = v
            else:
                for t, v in enumerate((hi, lo, hi)):
                    w3[s, m, pl.ds(t * 512, 512), pl.ds(k * 128, 128)] = v

    x_send(0, RW)
    for i, p in enumerate(peers):
        send(ew, ewb.at[h], hx_s.at[2 + i], hx_r.at[2 + i], (a, b, p))
        send(fb, fbb.at[h], hx_s.at[5 + i], hx_r.at[5 + i], (a, b, p))
    x_send(0, SW)
    x_send(0, OW)
    lanes = pl.ds(pl.multiple_of(h * Q2, Q2), Q2)
    for i, (g, q) in enumerate(around):
        send(ms.at[0, :, lanes], req.at[g, 1 - q], q_s.at[g, q + 1], q_r.at[g, 1 - q], dev(g, q))
    req[2, 1] = ms[0, :, lanes]
    ewb[h] = ew[...]
    fbb[h] = fb[...]

    load_grid.wait()
    for r in range(GROWS):
        base = (2 + r) * GCOLS
        wpack[pl.ds(2 * r, 2), :] = table[pl.ds(base, 2), :]
        epack[pl.ds(2 * r, 2), :] = table[pl.ds(base + GCOLS - 2, 2), :]
    for j, g in enumerate((0, 1, 2)):
        if g == 0:
            seg_at_target = 32 * (1 - core)
        elif g == 1:
            seg_at_target = 32 * core
        else:
            seg_at_target = 16
        for side_i, (pack, base, q) in enumerate(((epack, LEFT, 1), (wpack, RIGHT, -1))):
            send(
                pack, table.at[pl.ds(pl.multiple_of(base + seg_at_target, 16), 16)],
                hx_s.at[8 + 2 * j + side_i], hx_r.at[8 + 2 * j + side_i], dev(g, q),
            )

    x_forward(0, RW)

    local = (gr[0] - patch * NODES).astype(F32)
    node_rows = lax.broadcasted_iota(jnp.int32, (NODES, 128), 0).astype(F32)
    node_lanes = lax.broadcasted_iota(jnp.int32, (128, NODES), 1).astype(F32)

    def agg_block(row):
        return jnp.where(node_rows == row, 1.0, 0.0).astype(BF16)

    def sel_block(row):
        col = jnp.transpose(jnp.broadcast_to(row, (128, 128)))
        return jnp.where(node_lanes == jnp.concatenate([col] * 4, axis=1), 1.0, 0.0).astype(BF16)

    for j in range(E1 // 128):
        row = local[:, j * 128 : (j + 1) * 128]
        agg[:, pl.ds(j * 128, 128)] = agg_block(row)
        sel[pl.ds(j * 128, 128), :] = sel_block(row)

    x_forward(0, SW)
    y_forward(0, RW)
    x_forward(0, OW)
    y_forward(0, SW)
    for m in (RW, SW, OW):
        x_send(1, m)

    for i in range(3):
        arrived(ewb.at[peers[2 - i]], hx_r.at[2 + i], (a, b, peers[2 - i]))
        arrived(fbb.at[peers[2 - i]], hx_r.at[5 + i], (a, b, peers[2 - i]))

    def edge_weights(s):
        w = jnp.concatenate([ewb[k, s] for k in range(NHID)], axis=1)
        bias = jnp.concatenate([fbb[k, pl.ds(s, 1)] for k in range(NHID)], axis=1)
        wh = w.astype(BF16).astype(F32)
        bh = bias.astype(BF16).astype(F32)
        bl = (bias - bh).astype(BF16).astype(F32)
        bll = bias - bh - bl
        rows = [wh, w - wh, wh, bh, bl, bll, jnp.zeros_like(bll)]
        return jnp.concatenate(rows, axis=0).astype(BF16)

    def edge_feats(f):
        fh = f.astype(BF16).astype(F32)
        rows = [fh, fh, f - fh, jnp.ones_like(f)]
        return jnp.transpose(jnp.concatenate(rows, axis=0)).astype(BF16)

    ew0 = edge_weights(0)

    load_mesh.wait()
    c_wait(0, RW)
    build(0, RW)
    y_forward(0, OW)
    terms = dot(thrice(mid[...]), w3[0, RW])
    hi, lo = split(terms)
    r2[pl.ds(0, 512), :] = hi
    r2[pl.ds(512, 512), :] = lo

    c_wait(0, SW)
    build(0, SW)
    x_forward(1, RW)
    c_wait(0, OW)
    build(0, OW)
    x_forward(1, SW)

    to_smem.wait()
    arrived(low, hx_r.at[0], (down, b, h))
    arrived(high, hx_r.at[1], (up, b, h))
    for j, g in enumerate((0, 1, 2)):
        if g == 0:
            seg = 32 * core
        elif g == 1:
            seg = 32 * (1 - core)
        else:
            seg = 16
        for side_i, (base, q) in enumerate(((LEFT, -1), (RIGHT, 1))):
            arrived(
                table.at[pl.ds(pl.multiple_of(base + seg, 16), 16)],
                hx_r.at[8 + 2 * j + side_i], dev(g, q),
            )

    def take_rows(i, carry):
        for k in range(8):
            e = i * 8 + k
            xs[pl.ds(e, 1), :] = table[pl.ds(idx_s[0, e], 1), :]
        return carry

    lax.fori_loop(0, E1 // 8, take_rows, 0)
    x_forward(1, OW)
    y_forward(1, RW)

    STEP = 256
    for j in range(E1 // STEP):
        rows = pl.ds(j * STEP, STEP)
        one = sel[rows, :]
        pre = dot(thrice(xs[rows, :]), w3[0, SW])
        pre += dot(jnp.concatenate([one, one], axis=1), r2[...])
        pre += dot(edge_feats(gef[0, 0, :, j * STEP : (j + 1) * STEP]), ew0)
        hidden = silu(pre)
        message = dot(thrice(hidden), w3[0, OW]) + ob[pl.ds(0, 1), :]
        hi, lo = split(layer_norm(message, ng[pl.ds(0, 1), :], ns[pl.ds(0, 1), :]))
        nrm[rows, :] = hi
        nrm[pl.ds(E1 + j * STEP, STEP), :] = lo
        if j == 0:
            y_forward(1, SW)
        if j == 1:
            y_forward(1, OW)
        if j == 2:
            c_wait(1, SW)
            build(1, SW)

    both = agg[...]
    mid[...] += dot(jnp.concatenate([both, both], axis=1), nrm[...])
    mid3 = thrice(mid[...])
    hi, lo = split(dot(mid3, w3[1, SW]))
    r2[pl.ds(0, 512), :] = hi
    r2[pl.ds(512, 512), :] = lo

    for i, (g, q) in enumerate(around):
        arrived(req.at[g, q + 1], q_r.at[g, q + 1], dev(g, q))

    def contributions(g):
        picks = [sel_block((req[g, t] - patch * NODES).astype(F32)) for t in range(3)]
        picks = jnp.concatenate(picks, axis=0)
        found = dot(jnp.concatenate([picks, picks], axis=1), r2[...])
        for t in range(3):
            gbuf[g, t] = found[t * 128 : (t + 1) * 128]

    for g in range(2):
        contributions(g)
        for t in (0, 2, 1):
            send(gbuf.at[g, t], rlat.at[g, t], gl_s.at[g, t], gl_r.at[g, t], dev(g, 0))
    contributions(2)

    for m in (RW, OW):
        c_wait(1, m)
        build(1, m)
    local2 = (mr[0] - patch * NODES).astype(F32)
    for j in range(E2 // 128):
        agg[:, pl.ds(j * 128, 128)] = agg_block(local2[:, j * 128 : (j + 1) * 128])
    for k in range(NHID):
        midb[k] = mid[:, k * 128 : (k + 1) * 128]
    mine_recv = (mr[0, :, lanes] - patch * NODES).astype(F32)
    one = sel_block(mine_recv)
    mh, mlo = split(mid[...])
    picked = dot(one, mh) + dot(one, mlo)
    pre = dot(thrice(picked), w3[1, RW]) + dot(edge_feats(mef[0, 0, :, lanes]), edge_weights(1))

    for t, q in ((0, -1), (2, 1), (1, 0)):
        for g in (1, 0):
            arrived(rlat.at[g, t], gl_r.at[g, t], dev(g, 0))
        gbuf[2, t] = gbuf[2, t] + rlat[0, t] + rlat[1, t]
        if q != 0:
            send(gbuf.at[2, t], ry.at[1 if q < 0 else 0], gy_s.at[t], gy_r.at[1 if q < 0 else 0], dev(2, q))
    pre += gbuf[2, 1]
    arrived(ry.at[1], gy_r.at[1], dev(2, 1))
    arrived(ry.at[0], gy_r.at[0], dev(2, -1))
    pre += ry[0] + ry[1]
    message = dot(thrice(silu(pre)), w3[1, OW]) + ob[pl.ds(1, 1), :]
    normed = layer_norm(message, ng[pl.ds(1, 1), :], ns[pl.ds(1, 1), :])
    for k in range(NHID):
        n1[k] = normed[:, k * 128 : (k + 1) * 128]
    for i, p in enumerate(peers):
        send(n1.at[p], rm.at[h], a_s.at[i], a_r.at[i], (a, b, p))
    rm[h] = n1[h]
    for i in range(3):
        owner = peers[2 - i]
        arrived(rm.at[owner], a_r.at[i], (a, b, owner))
    hi, lo = split(rm[...].reshape(E2, 128))
    one = agg[:, pl.ds(0, E2)]
    out[0, 0] = midb[h] + dot(one, hi) + dot(one, lo)
    for copy in sent:
        copy.wait_send()


def per_device(gl, *rest):
    dma = pltpu.SemaphoreType.DMA
    vmem = pl.BlockSpec(memory_space=pltpu.VMEM)
    hbm = pl.BlockSpec(memory_space=pl.ANY)
    specs = [hbm, hbm, vmem, vmem, vmem, vmem, vmem, vmem, vmem, hbm, hbm, vmem, hbm, vmem, vmem, vmem]
    scratch = [
        pltpu.VMEM((TABLE, C), F32),
        pltpu.VMEM((NODES, C), F32),
        pltpu.VMEM((E1, C), F32),
        pltpu.VMEM((1, E1), jnp.int32),
        pltpu.SMEM((1, E1), jnp.int32),
        pltpu.VMEM((2, 2, NHID, 512, 128), F32),
        pltpu.VMEM((2, NHID, 128, 512), F32),
        pltpu.VMEM((2, 3, 1536, 512), BF16),
        pltpu.VMEM((1024, 512), BF16),
        pltpu.VMEM((E1, NODES), BF16),
        pltpu.VMEM((NODES, E1), BF16),
        pltpu.VMEM((2 * E1, C), BF16),
        pltpu.VMEM((NHID, 2, 4, 128), F32),
        pltpu.VMEM((NHID, 2, 128), F32),
        pltpu.VMEM((16, C), F32),
        pltpu.VMEM((16, C), F32),
        pltpu.VMEM((3, 3, 1, 128), jnp.int32),
        pltpu.VMEM((3, 3, 128, C), F32),
        pltpu.VMEM((2, 3, 128, C), F32),
        pltpu.VMEM((2, 128, C), F32),
        pltpu.VMEM((NHID, 128, 128), F32),
        pltpu.VMEM((NHID, 128, 128), F32),
        pltpu.VMEM((NHID, NODES, 128), F32),
        dma((9,)),
        dma((2, 3, 3)), dma((2, 3, 3)),
        dma((2, 3, 3, 2)), dma((2, 3, 3, 2)),
        dma((2, 3, 3, 2)), dma((2, 3, 3, 2)),
        dma((14,)), dma((14,)),
        dma((3, 3)), dma((3, 3)),
        dma((2, 3)), dma((2, 3)),
        dma((3,)), dma((2,)),
        dma((3,)), dma((3,)),
    ]
    return pl.pallas_call(
        kernel,
        out_shape=jax.ShapeDtypeStruct((1, 1, NODES, 128), F32),
        in_specs=specs,
        out_specs=vmem,
        scratch_shapes=scratch,
        compiler_params=pltpu.CompilerParams(
            collective_id=0, has_side_effects=True, vmem_limit_bytes=56 * 2**20
        ),
        cost_estimate=pl.CostEstimate(flops=10**10, bytes_accessed=10**7, transcendentals=10**6),
    )(gl.reshape(GROWS * GCOLS, C), *rest)


def solution(mesh):
    return jax.shard_map(
        per_device,
        mesh=mesh,
        in_specs=(
            P("lat", "lon", None),
            P("lat", "lon", None, None),
            P("lat", "lon", None, None),
            P("lat", "lon", None),
            P("lat", "lon", None),
            P("lat", "lon", None, None),
            P("lat", "lon", None),
            P("lat", "lon", None),
            P(None, None, "hid"),
            P(None, None, "hid"),
            P(None, None, "hid"),
            P(None, "hid"),
            P(None, "hid", None),
            P(),
            P(),
            P(),
        ),
        out_specs=P("lat", "lon", None, "hid"),
        check_vma=False,
    )
```

time: 185 us -> 70.7 us (0.38)
  the two profiles are of different devices: /device:TPU:192 before, /device:TPU:4 now
where the time goes in v1:
time: 70.7 us; the launch traced here: 70.5 us
  Pallas kernels  68.9 us (97%)
  local copies, waits for them, and re-layouts  1.67 us (2%)
    pallas_call x1, Pallas kernels, per_device(): pl.pallas_call(kernel, out_shape=jax.ShapeDtypeStruct((1, 1, NODES, 128),...  68.9 us
    unnamed x1, local copies, waits for them, and re-layouts  1.67 us

profile of v1, /device:TPU:4, one launch (start us, length us, event | category | flops | bytes accessed | tf_op | source)
XLA Modules:
  0.0 70.5 jit_solution(17477615976040853353)
XLA Ops:
  0.0 68.9 %shard_map.154 = f32[1,1,512,128]{3,2,1,0:T(8,128)} custom-call(f32[1024,512]{1,0:T(8,128)} %bitcast.1, f32[1,1,512,512]{3,2,1,0:T(8,128)} %ml.1, f32[1,1,4,1024]{3,2,1,0:T(4,128)} %gef.1, s32[1,1,1024]{2,1,0:T(1,128)} %gs.1, s32[1,1,1024]{2,1,0:T(1,128)} %gr.1, f32[1,1,4,512]{3,2,1,0:T(4,128)} %mef.1, s32[1,1,512]{2,1,0:T(1,128)} %ms.1, s32[1,1,512]{2,1,0:T(1,128)} %mr.1, ...), custom_call_target="tpu_custom_call" | custom-call | flops 10000000000 | bytes 10000000 | tf_op jit(solution)/shard_map/pallas_call | solution.py:441
  68.9 1.7 %copy.18 = f32[1,1,512,128]{3,2,1,0:T(8,128)} copy(f32[1,1,512,128]{3,2,1,0:T(8,128)} %shard_map.154) | data formatting | bytes 524288

commit v2 on v1

--- a/solution.py
+++ b/solution.py
@@ -50,9 +50,9 @@
     gl, ml, gef, gs, gr, mef, ms, mr, ew, sw, rw, fb, ow, ob, ng, ns,
     out,
     table, mid, xs, idx_v, idx_s, wcol, wout, w3, r2, sel, agg, nrm, ewb, fbb, epack, wpack,
-    req, gbuf, rlat, ry, n1, rm, midb,
+    req, gbuf, rlat, ry, rdiag, n1, rm, midb,
     load_sem, wx_s, wx_r, wy_s, wy_r, wc_s, wc_r, hx_s, hx_r, q_s, q_r, gl_s, gl_r, gy_s, gy_r,
-    a_s, a_r,
+    gd_s, gd_r, a_s, a_r,
 ):
     a = lax.axis_index("lat")
     b = lax.axis_index("lon")
@@ -228,6 +228,7 @@
             )
 
     x_forward(0, RW)
+    x_send(1, SW)
 
     local = (gr[0] - patch * NODES).astype(F32)
     node_rows = lax.broadcasted_iota(jnp.int32, (NODES, 128), 0).astype(F32)
@@ -246,11 +247,11 @@
         sel[pl.ds(j * 128, 128), :] = sel_block(row)
 
     x_forward(0, SW)
+    x_send(1, RW)
     y_forward(0, RW)
     x_forward(0, OW)
+    x_send(1, OW)
     y_forward(0, SW)
-    for m in (RW, SW, OW):
-        x_send(1, m)
 
     for i in range(3):
         arrived(ewb.at[peers[2 - i]], hx_r.at[2 + i], (a, b, peers[2 - i]))
@@ -284,10 +285,9 @@
 
     c_wait(0, SW)
     build(0, SW)
-    x_forward(1, RW)
+    x_forward(1, SW)
     c_wait(0, OW)
     build(0, OW)
-    x_forward(1, SW)
 
     to_smem.wait()
     arrived(low, hx_r.at[0], (down, b, h))
@@ -312,9 +312,6 @@
         return carry
 
     lax.fori_loop(0, E1 // 8, take_rows, 0)
-    x_forward(1, OW)
-    y_forward(1, RW)
-
     STEP = 256
     for j in range(E1 // STEP):
         rows = pl.ds(j * STEP, STEP)
@@ -330,13 +327,14 @@
         if j == 0:
             y_forward(1, SW)
         if j == 1:
-            y_forward(1, OW)
+            x_forward(1, RW)
         if j == 2:
-            c_wait(1, SW)
-            build(1, SW)
+            x_forward(1, OW)
 
     both = agg[...]
     mid[...] += dot(jnp.concatenate([both, both], axis=1), nrm[...])
+    c_wait(1, SW)
+    build(1, SW)
     mid3 = thrice(mid[...])
     hi, lo = split(dot(mid3, w3[1, SW]))
     r2[pl.ds(0, 512), :] = hi
@@ -352,11 +350,33 @@
         for t in range(3):
             gbuf[g, t] = found[t * 128 : (t + 1) * 128]
 
-    for g in range(2):
-        contributions(g)
-        for t in (0, 2, 1):
-            send(gbuf.at[g, t], rlat.at[g, t], gl_s.at[g, t], gl_r.at[g, t], dev(g, 0))
+    first, second = pl.ds(0, 64), pl.ds(64, 64)
+    contributions(0)
+    for t, q in ((0, -1), (2, 1)):
+        send(gbuf.at[0, t, first], rlat.at[0, t, first], gl_s.at[0, t, 0], gl_r.at[0, t, 0], dev(0, 0))
+        side_i = 1 if q < 0 else 0
+        send(gbuf.at[0, t, second], rdiag.at[side_i], gd_s.at[t], gd_r.at[side_i], dev(2, q))
+    send(gbuf.at[0, 1, first], rlat.at[0, 1, first], gl_s.at[0, 1, 0], gl_r.at[0, 1, 0], dev(0, 0))
+    contributions(1)
+    for t in (0, 2, 1):
+        send(gbuf.at[1, t], rlat.at[1, t], gl_s.at[1, t, 0], gl_r.at[1, t, 0], dev(1, 0))
     contributions(2)
+    for t, q in ((0, -1), (2, 1)):
+        arrived(rlat.at[1, t], gl_r.at[1, t, 0], dev(1, 0))
+        gbuf[2, t] = gbuf[2, t] + rlat[1, t]
+        side_i = 1 if q < 0 else 0
+        send(gbuf.at[2, t, second], ry.at[side_i, second], gy_s.at[t, 1], gy_r.at[side_i, 1], dev(2, q))
+    arrived(rdiag.at[1], gd_r.at[1], dev(2, 1))
+    arrived(rdiag.at[0], gd_r.at[0], dev(2, -1))
+    gbuf[0, 1, second] = gbuf[0, 1, second] + rdiag[0] + rdiag[1]
+    send(gbuf.at[0, 1, second], rlat.at[0, 1, second], gl_s.at[0, 1, 1], gl_r.at[0, 1, 1], dev(0, 0))
+    for t, q in ((0, -1), (2, 1)):
+        arrived(rlat.at[0, t, first], gl_r.at[0, t, 0], dev(0, 0))
+        gbuf[2, t, first] = gbuf[2, t, first] + rlat[0, t, first]
+        side_i = 1 if q < 0 else 0
+        send(gbuf.at[2, t, first], ry.at[side_i, first], gy_s.at[t, 0], gy_r.at[side_i, 0], dev(2, q))
+    y_forward(1, RW)
+    y_forward(1, OW)
 
     for m in (RW, OW):
         c_wait(1, m)
@@ -372,15 +392,13 @@
     picked = dot(one, mh) + dot(one, mlo)
     pre = dot(thrice(picked), w3[1, RW]) + dot(edge_feats(mef[0, 0, :, lanes]), edge_weights(1))
 
-    for t, q in ((0, -1), (2, 1), (1, 0)):
-        for g in (1, 0):
-            arrived(rlat.at[g, t], gl_r.at[g, t], dev(g, 0))
-        gbuf[2, t] = gbuf[2, t] + rlat[0, t] + rlat[1, t]
-        if q != 0:
-            send(gbuf.at[2, t], ry.at[1 if q < 0 else 0], gy_s.at[t], gy_r.at[1 if q < 0 else 0], dev(2, q))
-    pre += gbuf[2, 1]
-    arrived(ry.at[1], gy_r.at[1], dev(2, 1))
-    arrived(ry.at[0], gy_r.at[0], dev(2, -1))
+    arrived(rlat.at[1, 1], gl_r.at[1, 1, 0], dev(1, 0))
+    arrived(rlat.at[0, 1, first], gl_r.at[0, 1, 0], dev(0, 0))
+    arrived(rlat.at[0, 1, second], gl_r.at[0, 1, 1], dev(0, 0))
+    pre += gbuf[2, 1] + rlat[1, 1] + rlat[0, 1]
+    for part, rows in ((1, second), (0, first)):
+        arrived(ry.at[1, rows], gy_r.at[1, part], dev(2, 1))
+        arrived(ry.at[0, rows], gy_r.at[0, part], dev(2, -1))
     pre += ry[0] + ry[1]
     message = dot(thrice(silu(pre)), w3[1, OW]) + ob[pl.ds(1, 1), :]
     normed = layer_norm(message, ng[pl.ds(1, 1), :], ns[pl.ds(1, 1), :])
@@ -425,6 +443,7 @@
         pltpu.VMEM((3, 3, 128, C), F32),
         pltpu.VMEM((2, 3, 128, C), F32),
         pltpu.VMEM((2, 128, C), F32),
+        pltpu.VMEM((2, 64, C), F32),
         pltpu.VMEM((NHID, 128, 128), F32),
         pltpu.VMEM((NHID, 128, 128), F32),
         pltpu.VMEM((NHID, NODES, 128), F32),
@@ -434,7 +453,8 @@
         dma((2, 3, 3, 2)), dma((2, 3, 3, 2)),
         dma((14,)), dma((14,)),
         dma((3, 3)), dma((3, 3)),
-        dma((2, 3)), dma((2, 3)),
+        dma((2, 3, 2)), dma((2, 3, 2)),
+        dma((3, 2)), dma((2, 2)),
         dma((3,)), dma((2,)),
         dma((3,)), dma((3,)),
     ]

time: 70.7 us -> 64.6 us (0.914)
  the two profiles are of different devices: /device:TPU:4 before, /device:TPU:8 now
where the time goes in v2:
time: 64.6 us; the launch traced here: 64.4 us
  Pallas kernels  62.7 us (97%)
  local copies, waits for them, and re-layouts  1.67 us (3%)
    pallas_call x1, Pallas kernels, per_device(): pl.pallas_call(kernel, out_shape=jax.ShapeDtypeStruct((1, 1, NODES, 128),...  62.7 us
    unnamed x1, local copies, waits for them, and re-layouts  1.67 us

profile of v2, /device:TPU:8, one launch (start us, length us, event | category | flops | bytes accessed | tf_op | source)
XLA Modules:
  0.0 64.4 jit_solution(5061053698268954446)
XLA Ops:
  0.0 62.7 %shard_map.154 = f32[1,1,512,128]{3,2,1,0:T(8,128)} custom-call(f32[1024,512]{1,0:T(8,128)} %bitcast.1, f32[1,1,512,512]{3,2,1,0:T(8,128)} %ml.1, f32[1,1,4,1024]{3,2,1,0:T(4,128)} %gef.1, s32[1,1,1024]{2,1,0:T(1,128)} %gs.1, s32[1,1,1024]{2,1,0:T(1,128)} %gr.1, f32[1,1,4,512]{3,2,1,0:T(4,128)} %mef.1, s32[1,1,512]{2,1,0:T(1,128)} %ms.1, s32[1,1,512]{2,1,0:T(1,128)} %mr.1, ...), custom_call_target="tpu_custom_call" | custom-call | flops 10000000000 | bytes 10000000 | tf_op jit(solution)/shard_map/pallas_call | solution.py:461
  62.7 1.7 %copy.18 = f32[1,1,512,128]{3,2,1,0:T(8,128)} copy(f32[1,1,512,128]{3,2,1,0:T(8,128)} %shard_map.154) | data formatting | bytes 524288

commit v3 on v2

--- a/solution.py
+++ b/solution.py
@@ -49,7 +49,7 @@
 def kernel(
     gl, ml, gef, gs, gr, mef, ms, mr, ew, sw, rw, fb, ow, ob, ng, ns,
     out,
-    table, mid, xs, idx_v, idx_s, wcol, wout, w3, r2, sel, agg, nrm, ewb, fbb, epack, wpack,
+    table, mid, xs, idx_v, idx_s, wcol, wout, w3, r2, sel, agg, hidden, nrm, ewb, fbb, epack, wpack,
     req, gbuf, rlat, ry, rdiag, n1, rm, midb,
     load_sem, wx_s, wx_r, wy_s, wy_r, wc_s, wc_r, hx_s, hx_r, q_s, q_r, gl_s, gl_r, gy_s, gy_r,
     gd_s, gd_r, a_s, a_r,
@@ -247,48 +247,9 @@
         sel[pl.ds(j * 128, 128), :] = sel_block(row)
 
     x_forward(0, SW)
-    x_send(1, RW)
     y_forward(0, RW)
     x_forward(0, OW)
-    x_send(1, OW)
     y_forward(0, SW)
-
-    for i in range(3):
-        arrived(ewb.at[peers[2 - i]], hx_r.at[2 + i], (a, b, peers[2 - i]))
-        arrived(fbb.at[peers[2 - i]], hx_r.at[5 + i], (a, b, peers[2 - i]))
-
-    def edge_weights(s):
-        w = jnp.concatenate([ewb[k, s] for k in range(NHID)], axis=1)
-        bias = jnp.concatenate([fbb[k, pl.ds(s, 1)] for k in range(NHID)], axis=1)
-        wh = w.astype(BF16).astype(F32)
-        bh = bias.astype(BF16).astype(F32)
-        bl = (bias - bh).astype(BF16).astype(F32)
-        bll = bias - bh - bl
-        rows = [wh, w - wh, wh, bh, bl, bll, jnp.zeros_like(bll)]
-        return jnp.concatenate(rows, axis=0).astype(BF16)
-
-    def edge_feats(f):
-        fh = f.astype(BF16).astype(F32)
-        rows = [fh, fh, f - fh, jnp.ones_like(f)]
-        return jnp.transpose(jnp.concatenate(rows, axis=0)).astype(BF16)
-
-    ew0 = edge_weights(0)
-
-    load_mesh.wait()
-    c_wait(0, RW)
-    build(0, RW)
-    y_forward(0, OW)
-    terms = dot(thrice(mid[...]), w3[0, RW])
-    hi, lo = split(terms)
-    r2[pl.ds(0, 512), :] = hi
-    r2[pl.ds(512, 512), :] = lo
-
-    c_wait(0, SW)
-    build(0, SW)
-    x_forward(1, SW)
-    c_wait(0, OW)
-    build(0, OW)
-
     to_smem.wait()
     arrived(low, hx_r.at[0], (down, b, h))
     arrived(high, hx_r.at[1], (up, b, h))
@@ -312,6 +273,43 @@
         return carry
 
     lax.fori_loop(0, E1 // 8, take_rows, 0)
+
+    for i in range(3):
+        arrived(ewb.at[peers[2 - i]], hx_r.at[2 + i], (a, b, peers[2 - i]))
+        arrived(fbb.at[peers[2 - i]], hx_r.at[5 + i], (a, b, peers[2 - i]))
+
+    def edge_weights(s):
+        w = jnp.concatenate([ewb[k, s] for k in range(NHID)], axis=1)
+        bias = jnp.concatenate([fbb[k, pl.ds(s, 1)] for k in range(NHID)], axis=1)
+        wh = w.astype(BF16).astype(F32)
+        bh = bias.astype(BF16).astype(F32)
+        bl = (bias - bh).astype(BF16).astype(F32)
+        bll = bias - bh - bl
+        rows = [wh, w - wh, wh, bh, bl, bll, jnp.zeros_like(bll)]
+        return jnp.concatenate(rows, axis=0).astype(BF16)
+
+    def edge_feats(f):
+        fh = f.astype(BF16).astype(F32)
+        rows = [fh, fh, f - fh, jnp.ones_like(f)]
+        return jnp.transpose(jnp.concatenate(rows, axis=0)).astype(BF16)
+
+    ew0 = edge_weights(0)
+
+    load_mesh.wait()
+    c_wait(0, RW)
+    build(0, RW)
+    y_forward(0, OW)
+    terms = dot(thrice(mid[...]), w3[0, RW])
+    hi, lo = split(terms)
+    r2[pl.ds(0, 512), :] = hi
+    r2[pl.ds(512, 512), :] = lo
+
+    c_wait(0, SW)
+    build(0, SW)
+    x_forward(1, SW)
+    x_send(1, RW)
+    x_send(1, OW)
+
     STEP = 256
     for j in range(E1 // STEP):
         rows = pl.ds(j * STEP, STEP)
@@ -319,16 +317,21 @@
         pre = dot(thrice(xs[rows, :]), w3[0, SW])
         pre += dot(jnp.concatenate([one, one], axis=1), r2[...])
         pre += dot(edge_feats(gef[0, 0, :, j * STEP : (j + 1) * STEP]), ew0)
-        hidden = silu(pre)
-        message = dot(thrice(hidden), w3[0, OW]) + ob[pl.ds(0, 1), :]
+        hidden[0, rows, :], hidden[1, rows, :] = split(silu(pre))
+        if j == 1:
+            y_forward(1, SW)
+    c_wait(0, OW)
+    build(0, OW)
+    for j in range(E1 // STEP):
+        rows = pl.ds(j * STEP, STEP)
+        hi, lo = hidden[0, rows, :], hidden[1, rows, :]
+        message = dot(jnp.concatenate([hi, hi, lo], axis=1), w3[0, OW]) + ob[pl.ds(0, 1), :]
         hi, lo = split(layer_norm(message, ng[pl.ds(0, 1), :], ns[pl.ds(0, 1), :]))
         nrm[rows, :] = hi
         nrm[pl.ds(E1 + j * STEP, STEP), :] = lo
-        if j == 0:
-            y_forward(1, SW)
         if j == 1:
             x_forward(1, RW)
-        if j == 2:
+        if j == 3:
             x_forward(1, OW)
 
     both = agg[...]
@@ -377,7 +380,6 @@
         send(gbuf.at[2, t, first], ry.at[side_i, first], gy_s.at[t, 0], gy_r.at[side_i, 0], dev(2, q))
     y_forward(1, RW)
     y_forward(1, OW)
-
     for m in (RW, OW):
         c_wait(1, m)
         build(1, m)
@@ -392,24 +394,25 @@
     picked = dot(one, mh) + dot(one, mlo)
     pre = dot(thrice(picked), w3[1, RW]) + dot(edge_feats(mef[0, 0, :, lanes]), edge_weights(1))
 
+    pre += gbuf[2, 1]
     arrived(rlat.at[1, 1], gl_r.at[1, 1, 0], dev(1, 0))
-    arrived(rlat.at[0, 1, first], gl_r.at[0, 1, 0], dev(0, 0))
-    arrived(rlat.at[0, 1, second], gl_r.at[0, 1, 1], dev(0, 0))
-    pre += gbuf[2, 1] + rlat[1, 1] + rlat[0, 1]
     for part, rows in ((1, second), (0, first)):
+        arrived(rlat.at[0, 1, rows], gl_r.at[0, 1, part], dev(0, 0))
         arrived(ry.at[1, rows], gy_r.at[1, part], dev(2, 1))
         arrived(ry.at[0, rows], gy_r.at[0, part], dev(2, -1))
-    pre += ry[0] + ry[1]
-    message = dot(thrice(silu(pre)), w3[1, OW]) + ob[pl.ds(1, 1), :]
-    normed = layer_norm(message, ng[pl.ds(1, 1), :], ns[pl.ds(1, 1), :])
-    for k in range(NHID):
-        n1[k] = normed[:, k * 128 : (k + 1) * 128]
-    for i, p in enumerate(peers):
-        send(n1.at[p], rm.at[h], a_s.at[i], a_r.at[i], (a, b, p))
+        t = pre[part * 64 : part * 64 + 64]
+        t = t + rlat[1, 1, rows] + rlat[0, 1, rows] + ry[0, rows] + ry[1, rows]
+        message = dot(thrice(silu(t)), w3[1, OW]) + ob[pl.ds(1, 1), :]
+        normed = layer_norm(message, ng[pl.ds(1, 1), :], ns[pl.ds(1, 1), :])
+        for k in range(NHID):
+            n1[k, rows] = normed[:, k * 128 : (k + 1) * 128]
+        for i, p in enumerate(peers):
+            send(n1.at[p, rows], rm.at[h, rows], a_s.at[part, i], a_r.at[part, i], (a, b, p))
     rm[h] = n1[h]
-    for i in range(3):
-        owner = peers[2 - i]
-        arrived(rm.at[owner], a_r.at[i], (a, b, owner))
+    for part, rows in ((1, second), (0, first)):
+        for i in range(3):
+            owner = peers[2 - i]
+            arrived(rm.at[owner, rows], a_r.at[part, i], (a, b, owner))
     hi, lo = split(rm[...].reshape(E2, 128))
     one = agg[:, pl.ds(0, E2)]
     out[0, 0] = midb[h] + dot(one, hi) + dot(one, lo)
@@ -434,6 +437,7 @@
         pltpu.VMEM((1024, 512), BF16),
         pltpu.VMEM((E1, NODES), BF16),
         pltpu.VMEM((NODES, E1), BF16),
+        pltpu.VMEM((2, E1, C), BF16),
         pltpu.VMEM((2 * E1, C), BF16),
         pltpu.VMEM((NHID, 2, 4, 128), F32),
         pltpu.VMEM((NHID, 2, 128), F32),
@@ -456,7 +460,7 @@
         dma((2, 3, 2)), dma((2, 3, 2)),
         dma((3, 2)), dma((2, 2)),
         dma((3,)), dma((2,)),
-        dma((3,)), dma((3,)),
+        dma((2, 3)), dma((2, 3)),
     ]
     return pl.pallas_call(
         kernel,

time: 64.6 us -> 61.8 us (0.957)
  the two profiles are of different devices: /device:TPU:8 before, /device:TPU:16 now
where the time goes in v3:
time: 61.8 us; the launch traced here: 61.6 us
  Pallas kernels  59.9 us (97%)
  local copies, waits for them, and re-layouts  1.67 us (3%)
    pallas_call x1, Pallas kernels, per_device(): pl.pallas_call(kernel, out_shape=jax.ShapeDtypeStruct((1, 1, NODES, 128),...  59.9 us
    unnamed x1, local copies, waits for them, and re-layouts  1.67 us

profile of v3, /device:TPU:16, one launch (start us, length us, event | category | flops | bytes accessed | tf_op | source)
XLA Modules:
  0.0 61.6 jit_solution(114063366166045891)
XLA Ops:
  0.0 59.9 %shard_map.154 = f32[1,1,512,128]{3,2,1,0:T(8,128)} custom-call(f32[1024,512]{1,0:T(8,128)} %bitcast.1, f32[1,1,512,512]{3,2,1,0:T(8,128)} %ml.1, f32[1,1,4,1024]{3,2,1,0:T(4,128)} %gef.1, s32[1,1,1024]{2,1,0:T(1,128)} %gs.1, s32[1,1,1024]{2,1,0:T(1,128)} %gr.1, f32[1,1,4,512]{3,2,1,0:T(4,128)} %mef.1, s32[1,1,512]{2,1,0:T(1,128)} %ms.1, s32[1,1,512]{2,1,0:T(1,128)} %mr.1, ...), custom_call_target="tpu_custom_call" | custom-call | flops 10000000000 | bytes 10000000 | tf_op jit(solution)/shard_map/pallas_call | solution.py:465
  59.9 1.7 %copy.18 = f32[1,1,512,128]{3,2,1,0:T(8,128)} copy(f32[1,1,512,128]{3,2,1,0:T(8,128)} %shard_map.154) | data formatting | bytes 524288

commit v4 on v3

--- a/solution.py
+++ b/solution.py
@@ -298,7 +298,6 @@
     load_mesh.wait()
     c_wait(0, RW)
     build(0, RW)
-    y_forward(0, OW)
     terms = dot(thrice(mid[...]), w3[0, RW])
     hi, lo = split(terms)
     r2[pl.ds(0, 512), :] = hi
@@ -306,9 +305,7 @@
 
     c_wait(0, SW)
     build(0, SW)
-    x_forward(1, SW)
-    x_send(1, RW)
-    x_send(1, OW)
+    y_forward(0, OW)
 
     STEP = 256
     for j in range(E1 // STEP):
@@ -318,7 +315,11 @@
         pre += dot(jnp.concatenate([one, one], axis=1), r2[...])
         pre += dot(edge_feats(gef[0, 0, :, j * STEP : (j + 1) * STEP]), ew0)
         hidden[0, rows, :], hidden[1, rows, :] = split(silu(pre))
-        if j == 1:
+        if j == 0:
+            x_forward(1, SW)
+            x_send(1, RW)
+            x_send(1, OW)
+        if j == 3:
             y_forward(1, SW)
     c_wait(0, OW)
     build(0, OW)

time: 61.8 us -> 60.8 us (0.984)
  Pallas kernels: 59.9 us -> 58.9 us
    pallas_call x1, Pallas kernels: 59.9 us -> 58.9 us  [per_device(): pl.pallas_call(kernel, out_shape=jax.ShapeDtypeStruct((1, 1, NODES, 128),...]
where the time goes in v4:
time: 60.8 us; the launch traced here: 60.6 us
  Pallas kernels  58.9 us (97%)
  local copies, waits for them, and re-layouts  1.67 us (3%)
    pallas_call x1, Pallas kernels, per_device(): pl.pallas_call(kernel, out_shape=jax.ShapeDtypeStruct((1, 1, NODES, 128),...  58.9 us
    unnamed x1, local copies, waits for them, and re-layouts  1.67 us

profile of v4, /device:TPU:16, one launch (start us, length us, event | category | flops | bytes accessed | tf_op | source)
XLA Modules:
  0.0 60.6 jit_solution(6605994163326252737)
XLA Ops:
  0.0 58.9 %shard_map.154 = f32[1,1,512,128]{3,2,1,0:T(8,128)} custom-call(f32[1024,512]{1,0:T(8,128)} %bitcast.1, f32[1,1,512,512]{3,2,1,0:T(8,128)} %ml.1, f32[1,1,4,1024]{3,2,1,0:T(4,128)} %gef.1, s32[1,1,1024]{2,1,0:T(1,128)} %gs.1, s32[1,1,1024]{2,1,0:T(1,128)} %gr.1, f32[1,1,4,512]{3,2,1,0:T(4,128)} %mef.1, s32[1,1,512]{2,1,0:T(1,128)} %ms.1, s32[1,1,512]{2,1,0:T(1,128)} %mr.1, ...), custom_call_target="tpu_custom_call" | custom-call | flops 10000000000 | bytes 10000000 | tf_op jit(solution)/shard_map/pallas_call | solution.py:466
  58.9 1.7 %copy.18 = f32[1,1,512,128]{3,2,1,0:T(8,128)} copy(f32[1,1,512,128]{3,2,1,0:T(8,128)} %shard_map.154) | data formatting | bytes 524288
